TPU v7x, 32 devices: a whole 2x2x4 slice. The times are simulated.
32 devices in a mesh: row: 4 (over z), col: 4 (over y, x), section: 2 (over core).
Axes of the slice: x: 2, y: 2, z: 4, core: 2. Of those that a mesh axis runs over, the one named last changes fastest.
Arguments:
- hidden_in: bfloat16 [512, 8192], P(('col', 'section'), 'row'), may hold values from -6 to 6
- norm_gain: float32 [8192], P('row'), may hold values from 0.2 to 4
- gate_weight: bfloat16 [8192, 14336], P('row', ('col', 'section')), may hold values from -0.0625 to 0.0625
- up_weight: bfloat16 [8192, 14336], P('row', ('col', 'section')), may hold values from -0.0625 to 0.0625
- down_weight: bfloat16 [14336, 8192], P(('col', 'section'), 'row'), may hold values from -0.046875 to 0.046875
- proj_weight: bfloat16 [8192, 16384], P('row', ('col', 'section')), may hold values from -0.0625 to 0.0625
- teacher_out: bfloat16 [512, 16384], P(('row', 'col', 'section')), may hold values from -16 to 16
- loss_mask: int32 [512], P('row'), may hold values from 0 to 1, as said below
Outputs:
- loss_value: float32 [], replicated
- grad_gain: float32 [8192], P('row')
- grad_gate: float32 [8192, 14336], P('row', ('col', 'section'))
- grad_up: float32 [8192, 14336], P('row', ('col', 'section'))
- grad_down: float32 [14336, 8192], P(('col', 'section'), 'row')
- grad_proj: float32 [8192, 16384], P('row', ('col', 'section'))
- grad_input: float32 [512, 8192], P(('col', 'section'), 'row')
Inputs may be any that keep to these rules, and one draw needn't show every extreme that they name: `loss_mask`: the last token is always kept.
All inputs are finite; a program needn't handle non-finite values.
Results may differ from a plain program's by a relative error of at most 0.033.
Values may be sent and summed in bfloat16 or wider, within the bound.
No kernel may reach another device: no remote copies, remote signals or barrier semaphores. Data moves between devices by JAX's collectives and lax.ppermute only.
A program may use at most 192 MiB of HBM per device.

v0:
```python
import jax
import jax.numpy as jnp
from jax import lax
from jax.sharding import PartitionSpec as P

D = 8192


def contract_rows(left, right):
    return lax.dot_general(
        left, right, (((0,), (0,)), ((), ())), preferred_element_type=jnp.float32
    )


def contract_cols(left, right):
    return lax.dot_general(
        left, right, (((1,), (1,)), ((), ())), preferred_element_type=jnp.float32
    )


def silu_parts(gate_val):
    sigma = jax.nn.sigmoid(gate_val)
    return (gate_val * sigma, sigma)


def swiglu_back(hid_grad, gate_val, up_val):
    activated, sigma = silu_parts(gate_val)
    slope = sigma * (1.0 + gate_val * (1.0 - sigma))
    return (
        (hid_grad * up_val * slope).astype(jnp.bfloat16),
        (hid_grad * activated).astype(jnp.bfloat16),
    )


def body(
    hidden_in, norm_gain, gate_weight, up_weight, down_weight, proj_weight, teacher_out, loss_mask
):
    inputs = hidden_in.astype(jnp.float32)
    squares = lax.psum(jnp.sum(inputs * inputs, axis=1), "row")
    inv_rms = lax.rsqrt(squares / D + 1e-05)
    normed = (inputs * inv_rms[:, None] * norm_gain[None, :]).astype(jnp.bfloat16)
    normed_all = lax.all_gather(normed, ("col", "section"), axis=0, tiled=True)
    gate_val, up_val = (
        lax.psum(
            jnp.dot(normed_all, gate_weight, preferred_element_type=jnp.float32).astype(
                jnp.bfloat16
            ),
            "row",
        ).astype(jnp.float32),
        lax.psum(
            jnp.dot(normed_all, up_weight, preferred_element_type=jnp.float32).astype(jnp.bfloat16),
            "row",
        ).astype(jnp.float32),
    )
    activated, sigma = silu_parts(gate_val)
    hidden_all = (activated * up_val).astype(jnp.bfloat16)
    piece = hidden_all
    ffn_out = lax.psum_scatter(
        jnp.dot(piece, down_weight, preferred_element_type=jnp.float32).astype(jnp.bfloat16),
        ("col", "section"),
        scatter_dimension=0,
        tiled=True,
    ).astype(jnp.float32)
    residual = (inputs + ffn_out).astype(jnp.bfloat16)
    residual_all = lax.all_gather(residual, ("col", "section"), axis=0, tiled=True)
    piece = residual_all
    predicted = lax.psum_scatter(
        jnp.dot(piece, proj_weight, preferred_element_type=jnp.float32).astype(jnp.bfloat16),
        "row",
        scatter_dimension=0,
        tiled=True,
    ).astype(jnp.float32)
    target = lax.all_to_all(
        teacher_out, ("col", "section"), split_axis=1, concat_axis=0, tiled=True
    )
    keep = loss_mask.astype(jnp.float32)
    error = predicted - target.astype(jnp.float32)
    masked = error * keep[:, None]
    total_loss, total_count = lax.psum(
        (0.5 * jnp.sum(masked * error), jnp.sum(keep)), ("row", "col", "section")
    )
    loss_value = total_loss / (total_count / (lax.axis_size("col") * lax.axis_size("section")))
    pred_grad = masked.astype(jnp.bfloat16)
    pred_grad_all = lax.all_gather(pred_grad, "row", axis=0, tiled=True)
    grad_proj = contract_rows(residual_all, pred_grad_all)
    piece = pred_grad_all
    resid_grad = lax.psum_scatter(
        contract_cols(piece, proj_weight).astype(jnp.bfloat16),
        ("col", "section"),
        scatter_dimension=0,
        tiled=True,
    )
    resid_grad_all = lax.all_gather(resid_grad, ("col", "section"), axis=0, tiled=True)
    grad_down = contract_rows(hidden_all, resid_grad_all)
    hid_grad = lax.psum(
        contract_cols(resid_grad_all, down_weight).astype(jnp.bfloat16), "row"
    ).astype(jnp.float32)
    gate_grad, up_grad = swiglu_back(hid_grad, gate_val, up_val)
    grad_gate = contract_rows(normed_all, gate_grad)
    grad_up = contract_rows(normed_all, up_grad)
    normed_grad = lax.psum_scatter(
        (contract_cols(gate_grad, gate_weight) + contract_cols(up_grad, up_weight)).astype(
            jnp.bfloat16
        ),
        ("col", "section"),
        scatter_dimension=0,
        tiled=True,
    ).astype(jnp.float32)
    grad_gain = lax.psum(
        jnp.sum(normed_grad * inputs * inv_rms[:, None], axis=0), ("col", "section")
    )
    inner = lax.psum(jnp.sum(normed_grad * norm_gain[None, :] * inputs, axis=1), "row")
    grad_input = (
        resid_grad.astype(jnp.float32)
        + inv_rms[:, None] * (norm_gain[None, :] * normed_grad)
        - inputs * (inv_rms * inv_rms * inv_rms * inner / D)[:, None]
    )
    return (loss_value, grad_gain, grad_gate, grad_up, grad_down, grad_proj, grad_input)


def solution(mesh):
    in_specs = (
        P(("col", "section"), "row"),
        P("row"),
        P("row", ("col", "section")),
        P("row", ("col", "section")),
        P(("col", "section"), "row"),
        P("row", ("col", "section")),
        P(("row", "col", "section"), None),
        P("row"),
    )
    out_specs = (
        P(),
        P("row"),
        P("row", ("col", "section")),
        P("row", ("col", "section")),
        P(("col", "section"), "row"),
        P("row", ("col", "section")),
        P(("col", "section"), "row"),
    )
    return jax.shard_map(body, mesh=mesh, in_specs=in_specs, out_specs=out_specs, check_vma=False)
```

profile of v0, /device:TPU:0, one launch (start us, length us, event | category | flops | bytes accessed | tf_op | source)
XLA Modules:
  0.0 652.6 jit_solution(9415055318371113923)
XLA Ops:
  8.3 13.5 %psum.56 = f32[64]{0:T(128)S(1)} all-reduce(f32[64]{0:T(128)S(1)} %fusion.13), channel_id=1, replica_groups=mesh['row'=4,'col'=4,'section'=2] {'row'}, use_global_device_ids=true, to_apply=%region_1.0 | all-reduce | flops 64 | bytes 512 | tf_op jit(solution)/shard_map/psum | solution.py:39
  21.8 1.8 fusion.15
  23.6 26.2 %all-gather.5.cloned.1.call-done = bf16[512,2048]{1,0:T(8,128)(2,1)} async-done(((bf16[64,2048]{1,0:T(8,128)(2,1)}), bf16[512,2048]{1,0:T(8,128)(2,1)}) %all-gather.5.cloned.1.call-update) | async-done | bytes 2097168 | tf_op jit(solution)/shard_map/all_gather | solution.py:42
  49.9 9.0 %convolution_convert_fusion.4 = bf16[512,1792]{1,0:T(8,128)(2,1)} fusion(bf16[512,2048]{1,0:T(8,128)(2,1)} %all-gather.5.cloned.1.call-done, bf16[2048,1792]{1,0:T(8,128)(2,1)} %param.11), kind=kOutput, calls=%fused_computation.20 | convolution fusion | flops 3759013888 | bytes 11272192 | tf_op jit(solution)/shard_map/dot_general | solution.py:51
  58.9 8.2 %convolution_convert_fusion.5 = bf16[512,1792]{1,0:T(8,128)(2,1)} fusion(bf16[512,2048]{1,0:T(8,128)(2,1)S(1)} %copy-done.4, bf16[2048,1792]{1,0:T(8,128)(2,1)} %param.10), kind=kOutput, calls=%fused_computation.21 | convolution fusion | flops 3759013888 | bytes 11272192 | tf_op jit(solution)/shard_map/dot_general | solution.py:45
  67.2 138.5 %all-reduce.7.cloned.1.call-done = (bf16[512,1792]{1,0:T(8,128)(2,1)}, bf16[512,1792]{1,0:T(8,128)(2,1)}) async-done(((bf16[512,1792]{1,0:T(8,128)(2,1)}, bf16[512,1792]{1,0:T(8,128)(2,1)}), (bf16[512,1792]{1,0:T(8,128)(2,1)}, bf16[512,1792]{1,0:T(8,128)(2,1)})) %all-reduce.7.cloned.1.call-update) | async-done | bytes 3670032 | tf_op jit(solution)/shard_map/psum | solution.py:50
  205.7 9.8 %convolution_convert_fusion.3 = bf16[512,2048]{1,0:T(8,128)(2,1)} fusion(bf16[1792,2048]{1,0:T(8,128)(2,1)} %param.12, bf16[512,1792]{1,0:T(8,128)(2,1)} %get-tuple-element.11, bf16[512,1792]{1,0:T(8,128)(2,1)} %get-tuple-element.12), kind=kOutput, calls=%fused_computation.19 | convolution fusion | flops 3766484992 | bytes 13107200 | tf_op jit(solution)/shard_map/dot_general | solution.py:59
  215.5 40.3 %reduce-scatter.5.cloned.1.call-done = bf16[64,2048]{1,0:T(8,128)(2,1)} async-done(((bf16[512,2048]{1,0:T(8,128)(2,1)}), bf16[64,2048]{1,0:T(8,128)(2,1)}) %reduce-scatter.5.cloned.1.call-update) | async-done | bytes 262160 | tf_op jit(solution)/shard_map/reduce_scatter | solution.py:58
  255.9 1.7 fusion.16
  257.7 28.6 %all-gather.7.cloned.1.call-done = bf16[512,2048]{1,0:T(8,128)(2,1)} async-done(((bf16[64,2048]{1,0:T(8,128)(2,1)}), bf16[512,2048]{1,0:T(8,128)(2,1)}) %all-gather.7.cloned.1.call-update) | async-done | bytes 2097168 | tf_op jit(solution)/shard_map/all_gather | solution.py:65
  286.3 9.8 %convolution_convert_fusion.2 = bf16[512,2048]{1,0:T(8,128)(2,1)} fusion(bf16[512,2048]{1,0:T(8,128)(2,1)} %all-gather.7.cloned.1.call-done, bf16[2048,2048]{1,0:T(8,128)(2,1)} %param.13), kind=kOutput, calls=%fused_computation.18 | convolution fusion | flops 4296015872 | bytes 12582912 | tf_op jit(solution)/shard_map/dot_general | solution.py:68
  297.0 3.5 all-to-all-start
  300.7 9.4 %all-to-all-done = bf16[16,8,2048]{2,0,1:T(8,128)(2,1)S(1)} async-done(((bf16[16,8,2048]{2,0,1:T(8,128)(2,1)}), bf16[16,8,2048]{2,0,1:T(8,128)(2,1)S(1)}, u32[]{:S(2)}, u32[]{:S(2)}) %all-to-all-start) | async-done | bytes 524320 | tf_op jit(solution)/shard_map/all_to_all | solution.py:73
  310.2 30.0 %reduce-scatter.7.cloned.1.call-done = bf16[128,2048]{1,0:T(8,128)(2,1)} async-done(((bf16[512,2048]{1,0:T(8,128)(2,1)}), bf16[128,2048]{1,0:T(8,128)(2,1)}) %reduce-scatter.7.cloned.1.call-update) | async-done | bytes 524304 | tf_op jit(solution)/shard_map/reduce_scatter | solution.py:67
  340.2 2.7 multiply_convert_fusion
  342.9 45.4 %all-gather.9.cloned.1.call-done = bf16[512,2048]{1,0:T(8,128)(2,1)} async-done(((bf16[128,2048]{1,0:T(8,128)(2,1)}), bf16[512,2048]{1,0:T(8,128)(2,1)}) %all-gather.9.cloned.1.call-update) | async-done | bytes 2097168 | tf_op jit(solution)/shard_map/all_gather | solution.py:84
  388.3 9.9 %convolution_convert_fusion.1 = bf16[512,2048]{1,0:T(8,128)(2,1)} fusion(bf16[512,2048]{1,0:T(8,128)(2,1)} %all-gather.9.cloned.1.call-done, bf16[2048,2048]{1,0:T(8,128)(2,1)} %param.13), kind=kOutput, calls=%fused_computation.17 | convolution fusion | flops 4296015872 | bytes 12582912 | tf_op jit(solution)/shard_map/dot_general | solution.py:16
  398.2 40.0 %reduce-scatter.9.cloned.1.call-done = bf16[64,2048]{1,0:T(8,128)(2,1)} async-done(((bf16[512,2048]{1,0:T(8,128)(2,1)}), bf16[64,2048]{1,0:T(8,128)(2,1)}) %reduce-scatter.9.cloned.1.call-update) | async-done | bytes 262160 | tf_op jit(solution)/shard_map/reduce_scatter | solution.py:87
  438.3 29.9 %all-gather.11.cloned.1.call-done = bf16[512,2048]{1,0:T(8,128)(2,1)} async-done(((bf16[64,2048]{1,0:T(8,128)(2,1)}), bf16[512,2048]{1,0:T(8,128)(2,1)}) %all-gather.11.cloned.1.call-update) | async-done | bytes 2097168 | tf_op jit(solution)/shard_map/all_gather | solution.py:93
  468.2 8.9 %convolution_convert_fusion = bf16[512,1792]{1,0:T(8,128)(2,1)} fusion(bf16[512,2048]{1,0:T(8,128)(2,1)} %all-gather.11.cloned.1.call-done, bf16[1792,2048]{1,0:T(8,128)(2,1)} %param.12), kind=kOutput, calls=%fused_computation.16 | convolution fusion | flops 3759013888 | bytes 11272192 | tf_op jit(solution)/shard_map/dot_general | solution.py:16
  478.5 43.3 %all-reduce = (f32[]{:T(128)}, f32[]{:T(128)}) all-reduce(f32[]{:T(128)S(6)} %mul_shard_map.3, f32[]{:T(128)} %convert_reduce_fusion), channel_id=1, replica_groups=mesh['row'=4,'col'=4,'section'=2] {'row','col','section'}, use_global_device_ids=true, to_apply=%region_7.0 | all-reduce | flops 2 | bytes 16 | tf_op jit(solution)/shard_map/psum | solution.py:79
  523.1 13.1 %fusion.32 = f32[2048,2048]{1,0:T(8,128)} fusion(bf16[512,2048]{1,0:T(8,128)(2,1)} %all-gather.7.cloned.1.call-done, bf16[512,2048]{1,0:T(8,128)(2,1)} %all-gather.9.cloned.1.call-done), kind=kOutput, calls=%fused_computation.53 | convolution fusion | flops 4294967296 | bytes 20971520 | tf_op jit(solution)/shard_map/dot_general | solution.py:10
  536.2 19.9 %all-reduce.5.cloned.1.call-done = bf16[512,1792]{1,0:T(8,128)(2,1)} async-done(((bf16[512,1792]{1,0:T(8,128)(2,1)}), bf16[512,1792]{1,0:T(8,128)(2,1)}) %all-reduce.5.cloned.1.call-update) | async-done | bytes 1835024 | tf_op jit(solution)/shard_map/psum | solution.py:95
  556.1 10.4 %fusion.30 = f32[512,2048]{1,0:T(8,128)S(1)} fusion(bf16[2048,1792]{1,0:T(8,128)(2,1)} %param.10, bf16[512,1792]{1,0:T(8,128)(2,1)} %get-tuple-element.11, bf16[512,1792]{1,0:T(8,128)(2,1)} %all-reduce.5.cloned.1.call-done, bf16[512,1792]{1,0:T(8,128)(2,1)} %get-tuple-element.12), kind=kOutput, calls=%fused_computation.52 | convolution fusion | flops 3770023936 | bytes 17039360 | tf_op jit(solution)/shard_map/dot_general | solution.py:16
  566.5 8.8 %add_convert_fusion = bf16[512,2048]{1,0:T(8,128)(2,1)} fusion(f32[512,2048]{1,0:T(8,128)S(1)} %fusion.30, bf16[2048,1792]{1,0:T(8,128)(2,1)} %param.11, bf16[512,1792]{1,0:T(8,128)(2,1)S(1)} %copy-done.8, bf16[512,1792]{1,0:T(8,128)(2,1)S(1)} %copy-done.6), kind=kOutput, calls=%fused_computation.6 | convolution fusion | flops 3767533568 | bytes 17301504 | tf_op jit(solution)/shard_map/dot_general | solution.py:16
  575.3 12.6 %fusion.25 = f32[1792,2048]{1,0:T(8,128)} fusion(bf16[512,2048]{1,0:T(8,128)(2,1)} %all-gather.11.cloned.1.call-done, bf16[512,1792]{1,0:T(8,128)(2,1)} %get-tuple-element.11, bf16[512,1792]{1,0:T(8,128)(2,1)} %get-tuple-element.12), kind=kOutput, calls=%fused_computation.50 | convolution fusion | flops 3765436416 | bytes 20447232 | tf_op jit(solution)/shard_map/dot_general | solution.py:10
  588.0 7.8 %fusion.22 = f32[2048,1792]{1,0:T(8,128)} fusion(bf16[512,2048]{1,0:T(8,128)(2,1)S(1)} %copy-done.4, bf16[512,1792]{1,0:T(8,128)(2,1)S(1)} %copy-done.9, bf16[512,1792]{1,0:T(8,128)(2,1)S(1)} %copy-done.7), kind=kOutput, calls=%fused_computation.49 | convolution fusion | flops 3765436416 | bytes 20447232 | tf_op jit(solution)/shard_map/dot_general | solution.py:10
  595.7 7.9 %fusion.28 = f32[2048,1792]{1,0:T(8,128)} fusion(bf16[512,2048]{1,0:T(8,128)(2,1)S(1)} %copy-done.4, bf16[512,1792]{1,0:T(8,128)(2,1)S(1)} %copy-done.5, bf16[512,1792]{1,0:T(8,128)(2,1)S(1)} %copy-done.9, bf16[512,1792]{1,0:T(8,128)(2,1)S(1)} %copy-done.7), kind=kOutput, calls=%fused_computation.51 | convolution fusion | flops 3770023936 | bytes 22282240 | tf_op jit(solution)/shard_map/dot_general | solution.py:10
  603.7 12.1 %reduce-scatter.11.cloned.1.call-done = bf16[64,2048]{1,0:T(8,128)(2,1)} async-done(((bf16[512,2048]{1,0:T(8,128)(2,1)}), bf16[64,2048]{1,0:T(8,128)(2,1)}) %reduce-scatter.11.cloned.1.call-update) | async-done | bytes 262160 | tf_op jit(solution)/shard_map/reduce_scatter | solution.py:101
  617.0 13.6 %psum.62 = f32[2048]{0:T(1024)} all-reduce(f32[2048]{0:T(1024)S(1)} %get-tuple-element.8), channel_id=1, replica_groups=mesh['row'=4,'col'=4,'section'=2] {'col','section'}, use_global_device_ids=true, to_apply=%region_14.0 | all-reduce | flops 2048 | bytes 16384 | tf_op jit(solution)/shard_map/psum | solution.py:109
  630.5 11.7 %psum.63 = f32[64]{0:T(128)S(1)} all-reduce(f32[64]{0:T(128)S(1)} %get-tuple-element.7), channel_id=1, replica_groups=mesh['row'=4,'col'=4,'section'=2] {'row'}, use_global_device_ids=true, to_apply=%region_16.0 | all-reduce | flops 64 | bytes 512 | tf_op jit(solution)/shard_map/psum | solution.py:112
  642.2 2.0 fusion.12
  (49 shorter events, 4.6 us)
Async XLA Ops:
  7.2 42.7 %all-gather.5.cloned.1.call-start = ((), (), s32[]{:S(2)}) async-start(), calls=%async_computation.5 | async-start | bytes 2359296 | tf_op jit(solution)/shard_map/all_gather | solution.py:42
  23.6 182.1 %all-reduce.7.cloned.1.call-start = ((), (), s32[]{:S(2)}) async-start(), calls=%async_computation.14 | async-start | bytes 7340032 | tf_op jit(solution)/shard_map/psum | solution.py:50
  49.9 9.0 %copy-start.4 = (bf16[512,2048]{1,0:T(8,128)(2,1)S(1)}, bf16[512,2048]{1,0:T(8,128)(2,1)}, u32[]{:S(2)}) copy-start(bf16[512,2048]{1,0:T(8,128)(2,1)} %all-gather.5.cloned.1.call-done) | copy-start | bytes 6291460
  67.1 188.7 %reduce-scatter.5.cloned.1.call-start = ((), (), s32[]{:S(2)}) async-start(), calls=%async_computation.6 | async-start | bytes 2359296 | tf_op jit(solution)/shard_map/reduce_scatter | solution.py:58
  205.7 50.2 %copy-start = (bf16[64,2048]{1,0:T(8,128)(2,1)S(1)}, bf16[64,2048]{1,0:T(8,128)(2,1)}, u32[]{:S(2)}) copy-start(bf16[64,2048]{1,0:T(8,128)(2,1)} %param.8) | copy-start | bytes 786436
  215.5 70.8 %all-gather.7.cloned.1.call-start = ((), (), s32[]{:S(2)}) async-start(), calls=%async_computation.7 | async-start | bytes 2359296 | tf_op jit(solution)/shard_map/all_gather | solution.py:65
  257.6 38.5 %copy-start.2 = (bf16[16,16384]{1,0:T(8,128)(2,1)S(1)}, bf16[16,16384]{1,0:T(8,128)(2,1)}, u32[]{:S(2)}) copy-start(bf16[16,16384]{1,0:T(8,128)(2,1)} %param.14) | copy-start | bytes 1572868
  257.6 82.5 %reduce-scatter.7.cloned.1.call-start = ((), (), s32[]{:S(2)}) async-start(), calls=%async_computation.8 | async-start | bytes 2621440 | tf_op jit(solution)/shard_map/reduce_scatter | solution.py:67
  296.1 4.6 copy-start.10
  297.0 13.2 %all-to-all-start = ((bf16[16,8,2048]{2,0,1:T(8,128)(2,1)}), bf16[16,8,2048]{2,0,1:T(8,128)(2,1)S(1)}, u32[]{:S(2)}, u32[]{:S(2)}) async-start(bf16[16,8,2048]{2,0,1:T(8,128)(2,1)} %bitcast.29), calls=%async_computation.2 | async-start | bytes 1048576 | tf_op jit(solution)/shard_map/all_to_all | solution.py:73
  300.5 87.8 %all-gather.9.cloned.1.call-start = ((), (), s32[]{:S(2)}) async-start(), calls=%async_computation.9 | async-start | bytes 2621440 | tf_op jit(solution)/shard_map/all_gather | solution.py:84
  342.9 95.4 %reduce-scatter.9.cloned.1.call-start = ((), (), s32[]{:S(2)}) async-start(), calls=%async_computation.10 | async-start | bytes 2359296 | tf_op jit(solution)/shard_map/reduce_scatter | solution.py:87
  398.2 70.1 %all-gather.11.cloned.1.call-start = ((), (), s32[]{:S(2)}) async-start(), calls=%async_computation.11 | async-start | bytes 2359296 | tf_op jit(solution)/shard_map/all_gather | solution.py:93
  438.3 117.8 %all-reduce.5.cloned.1.call-start = ((), (), s32[]{:S(2)}) async-start(), calls=%async_computation.12 | async-start | bytes 3670016 | tf_op jit(solution)/shard_map/psum | solution.py:95
  477.2 138.6 %reduce-scatter.11.cloned.1.call-start = ((), (), s32[]{:S(2)}) async-start(), calls=%async_computation.13 | async-start | bytes 2359296 | tf_op jit(solution)/shard_map/reduce_scatter | solution.py:101
  556.1 10.4 %copy-start.6 = (bf16[512,1792]{1,0:T(8,128)(2,1)S(1)}, bf16[512,1792]{1,0:T(8,128)(2,1)}, u32[]{:S(2)}) copy-start(bf16[512,1792]{1,0:T(8,128)(2,1)} %get-tuple-element.12) | copy-start | bytes 5505028
  556.1 10.4 %copy-start.8 = (bf16[512,1792]{1,0:T(8,128)(2,1)S(1)}, bf16[512,1792]{1,0:T(8,128)(2,1)}, u32[]{:S(2)}) copy-start(bf16[512,1792]{1,0:T(8,128)(2,1)} %all-reduce.5.cloned.1.call-done) | copy-start | bytes 5505028
  575.3 12.6 %copy-start.7 = (bf16[512,1792]{1,0:T(8,128)(2,1)S(1)}, bf16[512,1792]{1,0:T(8,128)(2,1)}, u32[]{:S(2)}) copy-start(bf16[512,1792]{1,0:T(8,128)(2,1)} %get-tuple-element.12) | copy-start | bytes 5505028
  575.3 12.6 %copy-start.9 = (bf16[512,1792]{1,0:T(8,128)(2,1)S(1)}, bf16[512,1792]{1,0:T(8,128)(2,1)}, u32[]{:S(2)}) copy-start(bf16[512,1792]{1,0:T(8,128)(2,1)} %all-reduce.5.cloned.1.call-done) | copy-start | bytes 5505028
  588.0 7.8 %copy-start.5 = (bf16[512,1792]{1,0:T(8,128)(2,1)S(1)}, bf16[512,1792]{1,0:T(8,128)(2,1)}, u32[]{:S(2)}) copy-start(bf16[512,1792]{1,0:T(8,128)(2,1)} %get-tuple-element.11) | copy-start | bytes 5505028
  595.7 20.0 %copy-start.3 = (f32[2048]{0:T(1024)S(1)}, f32[2048]{0:T(1024)}, u32[]{:S(2)}) copy-start(f32[2048]{0:T(1024)} %param.9) | copy-start | bytes 24580
  595.7 46.5 %copy-start.1 = (bf16[64,2048]{1,0:T(8,128)(2,1)S(1)}, bf16[64,2048]{1,0:T(8,128)(2,1)}, u32[]{:S(2)}) copy-start(bf16[64,2048]{1,0:T(8,128)(2,1)} %reduce-scatter.9.cloned.1.call-done) | copy-start | bytes 786436
Sparse Core Ops, SparseCore 0:
  23.7 26.0 all-gather.4
  67.2 138.3 all-reduce.6
  215.6 40.2 reduce-scatter.4
  258.3 27.8 all-gather.6
  296.3 43.8 reduce-scatter.6
  343.0 45.2 all-gather.8
  398.3 39.9 reduce-scatter.8
  440.3 27.8 all-gather.10
  477.3 78.7 all-reduce.4
  575.4 40.2 reduce-scatter.10
where the time goes:
time: 661 us; the launch traced here: 653 us
  waiting for transfers between devices  420 us (64%)
  matrix products  116 us (18%)
  blocking collectives  82 us (12%)
  between operations  17.8 us (3%)
  other arithmetic  11.1 us (2%)
    psum x1, waiting for transfers between devices, body(): lax.psum(jnp.dot(normed_all, up_weight, preferred_element_type=jnp.float3...  138 us
    all_gather x1, waiting for transfers between devices, body(): pred_grad_all = lax.all_gather(pred_grad, 'row', axis=0, tiled=True)  45.4 us
    psum x1, blocking collectives, body(): lax.psum((0.5 * jnp.sum(masked * error), jnp.sum(keep)), ('row', 'col', '...  43.3 us
    dot_general x4, matrix products, contract_rows(): lax.dot_general(left, right, (((0,), (0,)), ((), ())), preferred_element_...  41.4 us
    reduce_scatter x1, waiting for transfers between devices, body(): lax.psum_scatter(jnp.dot(piece, down_weight, preferred_element_type=jnp.f...  40.3 us
    reduce_scatter x1, waiting for transfers between devices, body(): lax.psum_scatter(contract_cols(piece, proj_weight).astype(jnp.bfloat16),...  40 us
    dot_general x4, matrix products, contract_cols(): lax.dot_general(left, right, (((1,), (1,)), ((), ())), preferred_element_...  38 us
    reduce_scatter x1, waiting for transfers between devices, body(): lax.psum_scatter(jnp.dot(piece, proj_weight, preferred_element_type=jnp.f...  30 us
  transfers between devices with their start and end apart: 11, of which 11 were waited for; matrix products, arithmetic and copies ran while one was open for 7% of the time, Pallas kernels for 0%

commit v1 on v0

v1 whole, which is shorter than its diff:
```python
import jax
import jax.numpy as jnp
from jax import lax
from jax.sharding import PartitionSpec as P

PLANE = ("col", "section")
F32 = jnp.float32
BF16 = jnp.bfloat16


def mm(left, right):
    return jnp.dot(left, right, preferred_element_type=F32)


def mm_t(left, right):
    return lax.dot_general(left, right, (((1,), (1,)), ((), ())), preferred_element_type=F32)


def t_mm(left, right):
    return lax.dot_general(left, right, (((0,), (0,)), ((), ())), preferred_element_type=F32)


def reverse_bits(value, width):
    out = 0
    for bit in range(width):
        out |= ((value >> bit) & 1) << (width - 1 - bit)
    return out


class Plane:
    def __init__(self, size):
        self.size = size
        self.width = (size // 2).bit_length() - 1
        assert 2 << self.width == size
        self.rev = [reverse_bits(k, self.width) for k in range(size // 2)]
        self.perms = []
        for step in range(self.width):
            even, odd = 2 << step, 2 << (self.width - 1 - step)
            self.perms.append([(c, c ^ (odd if c & 1 else even)) for c in range(size)])
        self.swap = [(c, c ^ 1) for c in range(size)]

    def gather(self, block):
        own = block
        for perm in self.perms:
            own = jnp.concatenate([own, lax.ppermute(own, PLANE, perm)], axis=0)
        other = lax.ppermute(own, PLANE, self.swap)
        b = block.shape[0]
        parts = []
        for k in range(self.size // 2):
            j = self.rev[k]
            parts += [own[k * b : (k + 1) * b], other[j * b : (j + 1) * b]]
        return jnp.concatenate(parts, axis=0)

    def scatter(self, full):
        b = full.shape[0] // self.size
        block = lambda i: full[i * b : (i + 1) * b]
        half = self.size // 2
        mine = jnp.concatenate([block(2 * k) for k in range(half)], axis=0)
        send = jnp.concatenate([block(2 * self.rev[k] + 1) for k in range(half)], axis=0)
        got = lax.ppermute(send, PLANE, self.swap)
        acc = mine.astype(F32) + got.astype(F32)
        for perm in reversed(self.perms):
            half = acc.shape[0] // 2
            got = lax.ppermute(acc[half:].astype(BF16), PLANE, perm)
            acc = acc[:half] + got.astype(F32)
        return acc

    def total(self, value):
        for perm in self.perms + [self.swap]:
            value = value + lax.ppermute(value, PLANE, perm)
        return value


class Rows:
    def __init__(self, size, plane):
        self.size = size
        self.ring = [(r, (r + 1) % size) for r in range(size)]
        self.plane = plane
        self.me = lax.axis_index("row")
        c = lax.axis_index(PLANE)
        self.odd = (c & 1) == 1
        self.chip = c >> 1

    def owner(self, back):
        return lax.rem(self.me + (self.size - back), self.size)

    def start(self, owner, rows):
        k = self.chip ^ owner
        flipped = jnp.asarray(self.plane.rev, jnp.int32)[k]
        return jnp.where(self.odd, flipped, k) * rows

    def part(self, full, owner):
        rows = full.shape[0] // self.size
        return lax.dynamic_slice_in_dim(full, self.start(owner, rows), rows, 0)

    def place(self, full, block, owner):
        rows = block.shape[0]
        return lax.dynamic_update_slice_in_dim(full, block, self.start(owner, rows), 0)

    def shift(self, value):
        return lax.ppermute(value, "row", self.ring)

    def reduce(self, left, weights):
        got = None
        for back in range(1, self.size + 1):
            rows = self.part(left, self.owner(back))
            sums = [mm(rows, w) if not t else mm_t(rows, w) for w, t in weights]
            if got is not None:
                sums = [s + g.astype(F32) for s, g in zip(sums, got)]
            if back < self.size:
                got = [self.shift(s.astype(BF16)) for s in sums]
        return sums

    def gather(self, blocks, product):
        fulls, out = None, None
        for back in range(self.size):
            owner = self.owner(back)
            sent = [self.shift(b) for b in blocks] if back < self.size - 1 else None
            made = product(blocks)
            if fulls is None:
                fulls = [jnp.zeros((b.shape[0] * self.size,) + b.shape[1:], b.dtype) for b in blocks]
                out = jnp.zeros((made.shape[0] * self.size,) + made.shape[1:], made.dtype)
            fulls = [self.place(f, b, owner) for f, b in zip(fulls, blocks)]
            out = self.place(out, made, owner)
            blocks = sent
        return fulls, out

    def total(self, value):
        step = 1
        while step < self.size:
            value = value + lax.ppermute(value, "row", [(r, r ^ step) for r in range(self.size)])
            step *= 2
        return value

    def own_order(self, value):
        half = value.shape[0] // 2
        return jnp.where(self.odd, jnp.concatenate([value[half:], value[:half]], axis=0), value)


def make_body(n_row, n_plane):
    plane = Plane(n_plane)
    assert n_plane == 2 * n_row

    def body(x, gain, gate_w, up_w, down_w, proj_w, teacher, loss_mask):
        rows = Rows(n_row, plane)
        block = x.shape[0]
        features = x.shape[1] * n_row

        x_all = plane.gather(x)
        scaled = (x_all.astype(F32) * gain[None, :]).astype(BF16)
        squares = rows.total(jnp.sum(jnp.square(x_all.astype(F32)), axis=1))
        inv_all = lax.rsqrt(squares / features + 1e-05)
        inv = rows.part(inv_all, rows.me)[:, None]

        target = rows.own_order(
            lax.all_to_all(teacher, PLANE, split_axis=1, concat_axis=0, tiled=True)
        ).astype(F32)
        keep = rows.own_order(loss_mask.astype(F32))

        gate, up = rows.reduce(scaled, [(gate_w, False), (up_w, False)])
        gate, up = gate * inv, up * inv
        sigma = jax.nn.sigmoid(gate)
        activated = gate * sigma
        hidden = (activated * up).astype(BF16)
        (hidden_all,), ffn = rows.gather([hidden], lambda b: mm(b[0], down_w).astype(BF16))
        residual = (x.astype(F32) + plane.scatter(ffn)).astype(BF16)
        residual_all = plane.gather(residual)

        (predicted,) = rows.reduce(residual_all, [(proj_w, False)])
        error = predicted - target
        masked = error * keep[:, None]
        loss_parts = jnp.stack([0.5 * jnp.sum(masked * error), jnp.sum(keep)])
        loss_parts = rows.total(plane.total(loss_parts))
        loss_value = loss_parts[0] / (loss_parts[1] / n_plane)

        (pred_grad_all,), back = rows.gather(
            [masked.astype(BF16)], lambda b: mm_t(b[0], proj_w).astype(BF16)
        )
        grad_proj = t_mm(residual_all, pred_grad_all)
        resid_grad = plane.scatter(back).astype(BF16)
        resid_grad_all = plane.gather(resid_grad)
        grad_down = t_mm(hidden_all, resid_grad_all)

        (hid_grad,) = rows.reduce(resid_grad_all, [(down_w, True)])
        gate_grad = hid_grad * up * (sigma * (1.0 + gate * (1.0 - sigma)))
        up_grad = hid_grad * activated
        inner = rows.own_order(jnp.sum(gate_grad * gate + up_grad * up, axis=1))
        inner = plane.total(inner)
        (gate_grad_all, up_grad_all), back = rows.gather(
            [(gate_grad * inv).astype(BF16), (up_grad * inv).astype(BF16)],
            lambda b: (mm_t(b[0], gate_w) + mm_t(b[1], up_w)).astype(BF16),
        )
        grad_gate = t_mm(scaled, gate_grad_all)
        grad_up = t_mm(scaled, up_grad_all)
        grad_gain = plane.total(jnp.sum(back.astype(F32) * x_all.astype(F32), axis=0))
        normed_grad = plane.scatter(back)

        spread = jnp.zeros((n_row, inner.shape[0]), F32)
        spread = lax.dynamic_update_slice_in_dim(spread, inner[None, :], rows.me, 0)
        inner = lax.dynamic_slice_in_dim(
            rows.total(spread).reshape(-1), lax.axis_index(PLANE) * block, block, 0
        )
        inv_own = inv_all[:block]
        grad_input = (
            resid_grad.astype(F32)
            + gain[None, :] * normed_grad
            - x.astype(F32) * (inv_own * inv_own * inner / features)[:, None]
        )
        return (loss_value, grad_gain, grad_gate, grad_up, grad_down, grad_proj, grad_input)

    return body


def solution(mesh):
    in_specs = (
        P(PLANE, "row"),
        P("row"),
        P("row", PLANE),
        P("row", PLANE),
        P(PLANE, "row"),
        P("row", PLANE),
        P(("row", "col", "section"), None),
        P("row"),
    )
    out_specs = (
        P(),
        P("row"),
        P("row", PLANE),
        P("row", PLANE),
        P(PLANE, "row"),
        P("row", PLANE),
        P(PLANE, "row"),
    )
    body = make_body(mesh.shape["row"], mesh.shape["col"] * mesh.shape["section"])
    return jax.shard_map(body, mesh=mesh, in_specs=in_specs, out_specs=out_specs, check_vma=False)
```

time: 661 us -> 524 us (0.79)
  waiting for transfers between devices: 420 us -> 290 us
  blocking collectives: 82 us -> 0 us
  starting transfers between devices: 4.08 us -> 55.7 us
  local copies, waits for them, and re-layouts: 0.87 us -> 23 us
  between operations: 17.8 us -> 9.47 us
  matrix products: 116 us -> 123 us
    ppermute x0 -> x57, waiting for transfers between devices: none -> 290 us  [the longest x24 190 us: shift(): return lax.ppermute(value, 'row', self.ring)]
    psum x2 -> x0, waiting for transfers between devices: 158 us -> none  [the longest x1 138 us: body(): lax.psum(jnp.dot(normed_all, up_weight, preferred_element_type=jnp.float3...]
    all_gather x4 -> x0, waiting for transfers between devices: 130 us -> none  [the longest x1 45.4 us: body(): pred_grad_all = lax.all_gather(pred_grad, 'row', axis=0, tiled=True)]
    reduce_scatter x4 -> x0, waiting for transfers between devices: 122 us -> none  [the longest x1 40.3 us: body(): lax.psum_scatter(jnp.dot(piece, down_weight, preferred_element_type=jnp.f...]
    psum x4 -> x0, blocking collectives: 82 us -> none  [the longest x1 43.3 us: body(): lax.psum((0.5 * jnp.sum(masked * error), jnp.sum(keep)), ('row', 'col', '...]
    ppermute x0 -> x57, starting transfers between devices: none -> 52.2 us  [the longest x24 15.2 us: shift(): return lax.ppermute(value, 'row', self.ring)]
    unnamed x22 -> x119, local copies, waits for them, and re-layouts: 0.04 us -> 12.7 us
    all_to_all x1, waiting for transfers between devices: 9.43 us -> 0.01 us  [body(): lax.all_to_all(teacher, PLANE, split_axis=1, concat_axis=0, tiled=True)]
  transfers between devices with their start and end apart: 11 -> 58, of which waited for: 11 -> 43; matrix products, arithmetic and copies ran while one was open for 7% -> 21% of each run, Pallas kernels for 0% -> 0%
where the time goes in v1:
time: 524 us; the launch traced here: 515 us
  waiting for transfers between devices  290 us (55%)
  matrix products  123 us (23%)
  starting transfers between devices  55.7 us (11%)
  local copies, waits for them, and re-layouts  23 us (4%)
  other arithmetic  13.8 us (3%)
  between operations  9.47 us (2%)
    ppermute x24, waiting for transfers between devices, shift(): return lax.ppermute(value, 'row', self.ring)  190 us
    dot_general x16, matrix products, mm_t(): lax.dot_general(left, right, (((1,), (1,)), ((), ())), preferred_element_...  63.3 us
    ppermute x6, waiting for transfers between devices, gather(): own = jnp.concatenate([own, lax.ppermute(own, PLANE, perm)], axis=0)  38.8 us
    dot_general x4, matrix products, t_mm(): lax.dot_general(left, right, (((0,), (0,)), ((), ())), preferred_element_...  31.3 us
    dot_general x16, matrix products, mm(): return jnp.dot(left, right, preferred_element_type=F32)  28.4 us
    ppermute x6, waiting for transfers between devices, scatter(): got = lax.ppermute(acc[half:].astype(BF16), PLANE, perm)  27.1 us
    ppermute x6, waiting for transfers between devices, total(): lax.ppermute(value, 'row', [(r, r ^ step) for r in range(self.size)])  18.5 us
    ppermute x24, starting transfers between devices, shift(): return lax.ppermute(value, 'row', self.ring)  15.2 us
  transfers between devices with their start and end apart: 58, of which 43 were waited for; matrix products, arithmetic and copies ran while one was open for 21% of the time, Pallas kernels for 0%

profile of v1, /device:TPU:0, one launch (start us, length us, event | category | flops | bytes accessed | tf_op | source)
XLA Modules:
  0.0 515.2 jit_solution(8649929592118142240)
XLA Ops:
  11.3 7.2 %collective-permute-done.1 = bf16[128,2048]{1,0:T(8,128)(2,1)S(1)} collective-permute-done((bf16[128,2048]{1,0:T(8,128)(2,1)S(1)}, bf16[128,2048]{1,0:T(8,128)(2,1)S(1)}, u32[]{:S(2)}, u32[]{:S(2)}) %collective-permute-start.1) | collective-permute-done | bytes 524320 | tf_op jit(solution)/shard_map/ppermute | solution.py:45
  36.1 7.0 %collective-permute-done.7 = f32[512]{0:T(512)S(1)} collective-permute-done((f32[512]{0:T(512)S(1)}, f32[512]{0:T(512)S(1)}, u32[]{:S(2)}, u32[]{:S(2)}) %collective-permute-start.7) | collective-permute-done | bytes 2080 | tf_op jit(solution)/shard_map/ppermute | solution.py:131
  47.6 7.9 %collective-permute-done.8 = bf16[128,1792]{1,0:T(8,128)(2,1)S(1)} collective-permute-done((bf16[128,1792]{1,0:T(8,128)(2,1)S(1)}, bf16[128,1792]{1,0:T(8,128)(2,1)S(1)}, u32[]{:S(2)}, u32[]{:S(2)}) %collective-permute-start.8) | collective-permute-done | bytes 458784 | tf_op jit(solution)/shard_map/ppermute | solution.py:101
  56.8 8.6 %collective-permute-done.4 = bf16[128,1792]{1,0:T(8,128)(2,1)S(1)} collective-permute-done((bf16[128,1792]{1,0:T(8,128)(2,1)S(1)}, bf16[128,1792]{1,0:T(8,128)(2,1)S(1)}, u32[]{:S(2)}, u32[]{:S(2)}) %collective-permute-start.4) | collective-permute-done | bytes 458784 | tf_op jit(solution)/shard_map/ppermute | solution.py:101
  66.6 8.6 %collective-permute-done.9 = bf16[128,1792]{1,0:T(8,128)(2,1)S(1)} collective-permute-done((bf16[128,1792]{1,0:T(8,128)(2,1)S(1)}, bf16[128,1792]{1,0:T(8,128)(2,1)S(1)}, u32[]{:S(2)}, u32[]{:S(2)}) %collective-permute-start.9) | collective-permute-done | bytes 458784 | tf_op jit(solution)/shard_map/ppermute | solution.py:101
  76.4 8.6 %collective-permute-done.5 = bf16[128,1792]{1,0:T(8,128)(2,1)S(1)} collective-permute-done((bf16[128,1792]{1,0:T(8,128)(2,1)S(1)}, bf16[128,1792]{1,0:T(8,128)(2,1)S(1)}, u32[]{:S(2)}, u32[]{:S(2)}) %collective-permute-start.5) | collective-permute-done | bytes 458784 | tf_op jit(solution)/shard_map/ppermute | solution.py:101
  86.2 8.4 %collective-permute-done.10 = bf16[128,1792]{1,0:T(8,128)(2,1)S(1)} collective-permute-done((bf16[128,1792]{1,0:T(8,128)(2,1)S(1)}, bf16[128,1792]{1,0:T(8,128)(2,1)S(1)}, u32[]{:S(2)}, u32[]{:S(2)}) %collective-permute-start.10) | collective-permute-done | bytes 458784 | tf_op jit(solution)/shard_map/ppermute | solution.py:101
  99.3 12.0 %collective-permute-done.11 = bf16[128,1792]{1,0:T(8,128)(2,1)S(1)} collective-permute-done((bf16[128,1792]{1,0:T(8,128)(2,1)S(1)}, bf16[128,1792]{1,0:T(8,128)(2,1)S(1)}, u32[]{:S(2)}, u32[]{:S(2)}) %collective-permute-start.11) | collective-permute-done | bytes 458784 | tf_op jit(solution)/shard_map/ppermute | solution.py:101
  112.5 12.0 %collective-permute-done.12 = bf16[128,1792]{1,0:T(8,128)(2,1)S(1)} collective-permute-done((bf16[128,1792]{1,0:T(8,128)(2,1)S(1)}, bf16[128,1792]{1,0:T(8,128)(2,1)S(1)}, u32[]{:S(2)}, u32[]{:S(2)}) %collective-permute-start.12) | collective-permute-done | bytes 458784 | tf_op jit(solution)/shard_map/ppermute | solution.py:101
  125.6 11.0 %collective-permute-done.13 = bf16[128,1792]{1,0:T(8,128)(2,1)S(1)} collective-permute-done((bf16[128,1792]{1,0:T(8,128)(2,1)S(1)}, bf16[128,1792]{1,0:T(8,128)(2,1)S(1)}, u32[]{:S(2)}, u32[]{:S(2)}) %collective-permute-start.13) | collective-permute-done | bytes 458784 | tf_op jit(solution)/shard_map/ppermute | solution.py:101
  142.4 8.1 %collective-permute-done.15 = bf16[128,2048]{1,0:T(8,128)(2,1)S(1)} collective-permute-done((bf16[128,2048]{1,0:T(8,128)(2,1)S(1)}, bf16[128,2048]{1,0:T(8,128)(2,1)S(1)}, u32[]{:S(2)}, u32[]{:S(2)}) %collective-permute-start.15) | collective-permute-done | bytes 524320 | tf_op jit(solution)/shard_map/ppermute | solution.py:64
  164.9 8.1 %collective-permute-done.18 = bf16[128,2048]{1,0:T(8,128)(2,1)S(1)} collective-permute-done((bf16[128,2048]{1,0:T(8,128)(2,1)S(1)}, bf16[128,2048]{1,0:T(8,128)(2,1)S(1)}, u32[]{:S(2)}, u32[]{:S(2)}) %collective-permute-start.18) | collective-permute-done | bytes 524320 | tf_op jit(solution)/shard_map/ppermute | solution.py:45
  177.4 15.7 %collective-permute-done.20 = bf16[128,2048]{1,0:T(8,128)(2,1)S(1)} collective-permute-done((bf16[128,2048]{1,0:T(8,128)(2,1)S(1)}, bf16[128,2048]{1,0:T(8,128)(2,1)S(1)}, u32[]{:S(2)}, u32[]{:S(2)}) %collective-permute-start.20) | collective-permute-done | bytes 524320 | tf_op jit(solution)/shard_map/ppermute | solution.py:101
  199.0 10.5 %collective-permute-done.21 = bf16[128,2048]{1,0:T(8,128)(2,1)S(1)} collective-permute-done((bf16[128,2048]{1,0:T(8,128)(2,1)S(1)}, bf16[128,2048]{1,0:T(8,128)(2,1)S(1)}, u32[]{:S(2)}, u32[]{:S(2)}) %collective-permute-start.21) | collective-permute-done | bytes 524320 | tf_op jit(solution)/shard_map/ppermute | solution.py:101
  215.1 13.3 %collective-permute-done.22 = bf16[128,2048]{1,0:T(8,128)(2,1)S(1)} collective-permute-done((bf16[128,2048]{1,0:T(8,128)(2,1)S(1)}, bf16[128,2048]{1,0:T(8,128)(2,1)S(1)}, u32[]{:S(2)}, u32[]{:S(2)}) %collective-permute-start.22) | collective-permute-done | bytes 524320 | tf_op jit(solution)/shard_map/ppermute | solution.py:101
  243.3 6.5 %collective-permute-done.28 = bf16[128,2048]{1,0:T(8,128)(2,1)S(1)} collective-permute-done((bf16[128,2048]{1,0:T(8,128)(2,1)S(1)}, bf16[128,2048]{1,0:T(8,128)(2,1)S(1)}, u32[]{:S(2)}, u32[]{:S(2)}) %collective-permute-start.28) | collective-permute-done | bytes 524320 | tf_op jit(solution)/shard_map/ppermute | solution.py:101
  252.8 9.2 %collective-permute-done.29 = bf16[128,2048]{1,0:T(8,128)(2,1)S(1)} collective-permute-done((bf16[128,2048]{1,0:T(8,128)(2,1)S(1)}, bf16[128,2048]{1,0:T(8,128)(2,1)S(1)}, u32[]{:S(2)}, u32[]{:S(2)}) %collective-permute-start.29) | collective-permute-done | bytes 524320 | tf_op jit(solution)/shard_map/ppermute | solution.py:101
  262.0 8.3 %collective-permute-start.30 = (bf16[128,2048]{1,0:T(8,128)(2,1)S(1)}, bf16[128,2048]{1,0:T(8,128)(2,1)S(1)}, u32[]{:S(2)}, u32[]{:S(2)}) collective-permute-start(bf16[128,2048]{1,0:T(8,128)(2,1)S(1)} %collective-permute-done.29), channel_id=1, source_target_pairs={{0,8},{8,16},{16,24},{24,0},{1,9},{9,17},{17,25},{25,1},{2,10},{10... | collective-permute-start | bytes 1572872 | tf_op jit(solution)/shard_map/ppermute | solution.py:101
  273.2 8.3 %collective-permute-done.30 = bf16[128,2048]{1,0:T(8,128)(2,1)S(1)} collective-permute-done((bf16[128,2048]{1,0:T(8,128)(2,1)S(1)}, bf16[128,2048]{1,0:T(8,128)(2,1)S(1)}, u32[]{:S(2)}, u32[]{:S(2)}) %collective-permute-start.30) | collective-permute-done | bytes 524320 | tf_op jit(solution)/shard_map/ppermute | solution.py:101
  289.0 8.2 %collective-permute-done.32 = bf16[128,2048]{1,0:T(8,128)(2,1)S(1)} collective-permute-done((bf16[128,2048]{1,0:T(8,128)(2,1)S(1)}, bf16[128,2048]{1,0:T(8,128)(2,1)S(1)}, u32[]{:S(2)}, u32[]{:S(2)}) %collective-permute-start.32) | collective-permute-done | bytes 524320 | tf_op jit(solution)/shard_map/ppermute | solution.py:64
  312.1 8.2 %collective-permute-done.35 = bf16[128,2048]{1,0:T(8,128)(2,1)S(1)} collective-permute-done((bf16[128,2048]{1,0:T(8,128)(2,1)S(1)}, bf16[128,2048]{1,0:T(8,128)(2,1)S(1)}, u32[]{:S(2)}, u32[]{:S(2)}) %collective-permute-start.35) | collective-permute-done | bytes 524320 | tf_op jit(solution)/shard_map/ppermute | solution.py:45
  329.2 6.7 %convolution_convert_fusion.5 = bf16[128,1792]{1,0:T(8,128)(2,1)} fusion(bf16[1792,2048]{1,0:T(8,128)(2,1)} %param.53, bf16[512,2048]{1,0:T(8,128)(2,1)} %slice_dynamic-update-slice_fusion, s32[]{:T(128)S(6)} %select_n.337), kind=kOutput, calls=%fused_computation.38 | convolution fusion | flops 939753472 | bytes 8323076 | tf_op jit(solution)/shard_map/dot_general | solution.py:16
  343.5 7.1 %collective-permute-done.37 = bf16[128,1792]{1,0:T(8,128)(2,1)} collective-permute-done((bf16[128,1792]{1,0:T(8,128)(2,1)}, bf16[128,1792]{1,0:T(8,128)(2,1)}, u32[]{:S(2)}, u32[]{:S(2)}) %collective-permute-start.37) | collective-permute-done | bytes 458784 | tf_op jit(solution)/shard_map/ppermute | solution.py:101
  358.4 7.7 %collective-permute-done.26 = f32[2]{0:T(128)S(1)} collective-permute-done((f32[2]{0:T(128)S(1)}, f32[2]{0:T(128)S(1)}, u32[]{:S(2)}, u32[]{:S(2)}) %collective-permute-start.26) | collective-permute-done | bytes 40 | tf_op jit(solution)/shard_map/ppermute | solution.py:131
  378.0 10.7 %collective-permute-done.39 = bf16[128,1792]{1,0:T(8,128)(2,1)S(1)} collective-permute-done((bf16[128,1792]{1,0:T(8,128)(2,1)S(1)}, bf16[128,1792]{1,0:T(8,128)(2,1)S(1)}, u32[]{:S(2)}, u32[]{:S(2)}) %collective-permute-start.39) | collective-permute-done | bytes 458784 | tf_op jit(solution)/shard_map/ppermute | solution.py:101
  394.7 8.6 %fusion.100 = f32[2048,2048]{1,0:T(8,128)} fusion(bf16[512,2048]{1,0:T(8,128)(2,1)S(1)} %copy-done.13, bf16[512,2048]{1,0:T(8,128)(2,1)S(1)} %constant_dynamic-update-slice_fusion.21), kind=kOutput, calls=%fused_computation.201 | convolution fusion | flops 4294967296 | bytes 20971520 | tf_op jit(solution)/shard_map/dot_general | solution.py:20
  404.5 7.6 %fusion.99 = f32[1792,2048]{1,0:T(8,128)} fusion(bf16[512,1792]{1,0:T(8,128)(2,1)S(1)} %copy-done.27, bf16[512,2048]{1,0:T(8,128)(2,1)S(1)} %copy-done.28), kind=kOutput, calls=%fused_computation.200 | convolution fusion | flops 3758096384 | bytes 18612224 | tf_op jit(solution)/shard_map/dot_general | solution.py:20
  415.7 6.8 %fusion.93 = f32[128,2048]{1,0:T(8,128)} fusion(bf16[128,1792]{1,0:T(8,128)(2,1)} %get-tuple-element.14, bf16[2048,1792]{1,0:T(8,128)(2,1)} %param.51), kind=kOutput, calls=%fused_computation.194 | convolution fusion | flops 939524096 | bytes 8847360 | tf_op jit(solution)/shard_map/dot_general | solution.py:16
  457.4 7.4 %collective-permute-done.42 = bf16[128,1792]{1,0:T(8,128)(2,1)S(1)} collective-permute-done((bf16[128,1792]{1,0:T(8,128)(2,1)}, bf16[128,1792]{1,0:T(8,128)(2,1)S(1)}, u32[]{:S(2)}, u32[]{:S(2)}) %collective-permute-start.42) | collective-permute-done | bytes 458784 | tf_op jit(solution)/shard_map/ppermute | solution.py:101
  467.3 7.3 %collective-permute-done.45 = bf16[128,1792]{1,0:T(8,128)(2,1)S(1)} collective-permute-done((bf16[128,1792]{1,0:T(8,128)(2,1)S(1)}, bf16[128,1792]{1,0:T(8,128)(2,1)S(1)}, u32[]{:S(2)}, u32[]{:S(2)}) %collective-permute-start.45) | collective-permute-done | bytes 458784 | tf_op jit(solution)/shard_map/ppermute | solution.py:101
  492.3 7.6 %fusion.98 = f32[2048,1792]{1,0:T(8,128)} fusion(bf16[512,2048]{1,0:T(8,128)(2,1)S(1)} %copy-done.2, bf16[512,1792]{1,0:T(8,128)(2,1)S(1)} %constant_dynamic-update-slice_fusion.18), kind=kOutput, calls=%fused_computation.199 | convolution fusion | flops 3758096384 | bytes 18612224 | tf_op jit(solution)/shard_map/dot_general | solution.py:20
  504.5 7.6 %fusion.97 = f32[2048,1792]{1,0:T(8,128)} fusion(bf16[512,2048]{1,0:T(8,128)(2,1)S(1)} %copy-done.2, bf16[512,1792]{1,0:T(8,128)(2,1)S(1)} %constant_dynamic-update-slice_fusion.8), kind=kOutput, calls=%fused_computation.198 | convolution fusion | flops 3758096384 | bytes 18612224 | tf_op jit(solution)/shard_map/dot_general | solution.py:20
  (330 shorter events, 225.1 us)
Async XLA Ops:
  30.1 15.6 %collective-permute-start.3 = (bf16[128,1792]{1,0:T(8,128)(2,1)S(1)}, bf16[128,1792]{1,0:T(8,128)(2,1)S(1)}, u32[]{:S(2)}, u32[]{:S(2)}) collective-permute-start(bf16[128,1792]{1,0:T(8,128)(2,1)S(1)} %convolution_convert_fusion.11), channel_id=1, source_target_pairs={{0,8},{8,16},{16,24},{24,0},{1,9},{9,17},{17,25},{25,1},{2,10},{10... | collective-permute-start | bytes 1376264 | tf_op jit(solution)/shard_map/ppermute | solution.py:101
  32.2 10.9 %collective-permute-start.7 = (f32[512]{0:T(512)S(1)}, f32[512]{0:T(512)S(1)}, u32[]{:S(2)}, u32[]{:S(2)}) collective-permute-start(f32[512]{0:T(512)S(1)} %add.370), channel_id=1, source_target_pairs={{0,16},{8,24},{16,0},{24,8},{1,17},{9,25},{17,1},{25,9},{2,18},{10... | collective-permute-start | bytes 6152 | tf_op jit(solution)/shard_map/ppermute | solution.py:131
  36.0 19.5 %collective-permute-start.8 = (bf16[128,1792]{1,0:T(8,128)(2,1)S(1)}, bf16[128,1792]{1,0:T(8,128)(2,1)S(1)}, u32[]{:S(2)}, u32[]{:S(2)}) collective-permute-start(bf16[128,1792]{1,0:T(8,128)(2,1)S(1)} %convolution_convert_fusion.10), channel_id=1, source_target_pairs={{0,8},{8,16},{16,24},{24,0},{1,9},{9,17},{17,25},{25,1},{2,10},{10... | collective-permute-start | bytes 1376264 | tf_op jit(solution)/shard_map/ppermute | solution.py:101
  46.8 18.5 %collective-permute-start.4 = (bf16[128,1792]{1,0:T(8,128)(2,1)S(1)}, bf16[128,1792]{1,0:T(8,128)(2,1)S(1)}, u32[]{:S(2)}, u32[]{:S(2)}) collective-permute-start(bf16[128,1792]{1,0:T(8,128)(2,1)S(1)} %add_convert_fusion.3), channel_id=1, source_target_pairs={{0,8},{8,16},{16,24},{24,0},{1,9},{9,17},{17,25},{25,1},{2,10},{10... | collective-permute-start | bytes 1376264 | tf_op jit(solution)/shard_map/ppermute | solution.py:101
  56.7 18.5 %collective-permute-start.9 = (bf16[128,1792]{1,0:T(8,128)(2,1)S(1)}, bf16[128,1792]{1,0:T(8,128)(2,1)S(1)}, u32[]{:S(2)}, u32[]{:S(2)}) collective-permute-start(bf16[128,1792]{1,0:T(8,128)(2,1)S(1)} %add_convert_fusion.1), channel_id=1, source_target_pairs={{0,8},{8,16},{16,24},{24,0},{1,9},{9,17},{17,25},{25,1},{2,10},{10... | collective-permute-start | bytes 1376264 | tf_op jit(solution)/shard_map/ppermute | solution.py:101
  66.5 18.5 %collective-permute-start.5 = (bf16[128,1792]{1,0:T(8,128)(2,1)S(1)}, bf16[128,1792]{1,0:T(8,128)(2,1)S(1)}, u32[]{:S(2)}, u32[]{:S(2)}) collective-permute-start(bf16[128,1792]{1,0:T(8,128)(2,1)S(1)} %add_convert_fusion.2), channel_id=1, source_target_pairs={{0,8},{8,16},{16,24},{24,0},{1,9},{9,17},{17,25},{25,1},{2,10},{10... | collective-permute-start | bytes 1376264 | tf_op jit(solution)/shard_map/ppermute | solution.py:101
  76.4 18.2 %collective-permute-start.10 = (bf16[128,1792]{1,0:T(8,128)(2,1)S(1)}, bf16[128,1792]{1,0:T(8,128)(2,1)S(1)}, u32[]{:S(2)}, u32[]{:S(2)}) collective-permute-start(bf16[128,1792]{1,0:T(8,128)(2,1)S(1)} %add_convert_fusion), channel_id=1, source_target_pairs={{0,8},{8,16},{16,24},{24,0},{1,9},{9,17},{17,25},{25,1},{2,10},{10... | collective-permute-start | bytes 1376264 | tf_op jit(solution)/shard_map/ppermute | solution.py:101
  97.1 14.3 %collective-permute-start.11 = (bf16[128,1792]{1,0:T(8,128)(2,1)S(1)}, bf16[128,1792]{1,0:T(8,128)(2,1)S(1)}, u32[]{:S(2)}, u32[]{:S(2)}) collective-permute-start(bf16[128,1792]{1,0:T(8,128)(2,1)S(1)} %get-tuple-element.10), channel_id=1, source_target_pairs={{0,8},{8,16},{16,24},{24,0},{1,9},{9,17},{17,25},{25,1},{2,10},{10... | collective-permute-start | bytes 1376264 | tf_op jit(solution)/shard_map/ppermute | solution.py:101
  111.3 13.1 %collective-permute-start.12 = (bf16[128,1792]{1,0:T(8,128)(2,1)S(1)}, bf16[128,1792]{1,0:T(8,128)(2,1)S(1)}, u32[]{:S(2)}, u32[]{:S(2)}) collective-permute-start(bf16[128,1792]{1,0:T(8,128)(2,1)S(1)} %collective-permute-done.11), channel_id=1, source_target_pairs={{0,8},{8,16},{16,24},{24,0},{1,9},{9,17},{17,25},{25,1},{2,10},{10... | collective-permute-start | bytes 1376264 | tf_op jit(solution)/shard_map/ppermute | solution.py:101
  124.4 12.2 %collective-permute-start.13 = (bf16[128,1792]{1,0:T(8,128)(2,1)S(1)}, bf16[128,1792]{1,0:T(8,128)(2,1)S(1)}, u32[]{:S(2)}, u32[]{:S(2)}) collective-permute-start(bf16[128,1792]{1,0:T(8,128)(2,1)S(1)} %collective-permute-done.12), channel_id=1, source_target_pairs={{0,8},{8,16},{16,24},{24,0},{1,9},{9,17},{17,25},{25,1},{2,10},{10... | collective-permute-start | bytes 1376264 | tf_op jit(solution)/shard_map/ppermute | solution.py:101
  177.4 15.8 %collective-permute-start.20 = (bf16[128,2048]{1,0:T(8,128)(2,1)S(1)}, bf16[128,2048]{1,0:T(8,128)(2,1)S(1)}, u32[]{:S(2)}, u32[]{:S(2)}) collective-permute-start(bf16[128,2048]{1,0:T(8,128)(2,1)S(1)} %convolution_convert_fusion.4), channel_id=1, source_target_pairs={{0,8},{8,16},{16,24},{24,0},{1,9},{9,17},{17,25},{25,1},{2,10},{10... | collective-permute-start | bytes 1572872 | tf_op jit(solution)/shard_map/ppermute | solution.py:101
  194.5 15.0 %collective-permute-start.21 = (bf16[128,2048]{1,0:T(8,128)(2,1)S(1)}, bf16[128,2048]{1,0:T(8,128)(2,1)S(1)}, u32[]{:S(2)}, u32[]{:S(2)}) collective-permute-start(bf16[128,2048]{1,0:T(8,128)(2,1)S(1)} %fusion.19), channel_id=1, source_target_pairs={{0,8},{8,16},{16,24},{24,0},{1,9},{9,17},{17,25},{25,1},{2,10},{10... | collective-permute-start | bytes 1572872 | tf_op jit(solution)/shard_map/ppermute | solution.py:101
  195.4 19.7 %all-to-all-start = ((bf16[16,8,2048]{2,0,1:T(8,128)(2,1)}), bf16[16,8,2048]{2,0,1:T(8,128)(2,1)S(1)}, u32[]{:S(2)}, u32[]{:S(2)}) async-start(bf16[16,8,2048]{2,0,1:T(8,128)(2,1)} %bitcast.77), calls=%async_computation | async-start | bytes 1048576 | tf_op jit(solution)/shard_map/all_to_all | solution.py:156
  214.3 14.1 %collective-permute-start.22 = (bf16[128,2048]{1,0:T(8,128)(2,1)S(1)}, bf16[128,2048]{1,0:T(8,128)(2,1)S(1)}, u32[]{:S(2)}, u32[]{:S(2)}) collective-permute-start(bf16[128,2048]{1,0:T(8,128)(2,1)S(1)} %fusion.18), channel_id=1, source_target_pairs={{0,8},{8,16},{16,24},{24,0},{1,9},{9,17},{17,25},{25,1},{2,10},{10... | collective-permute-start | bytes 1572872 | tf_op jit(solution)/shard_map/ppermute | solution.py:101
  236.7 13.1 %collective-permute-start.28 = (bf16[128,2048]{1,0:T(8,128)(2,1)S(1)}, bf16[128,2048]{1,0:T(8,128)(2,1)S(1)}, u32[]{:S(2)}, u32[]{:S(2)}) collective-permute-start(bf16[128,2048]{1,0:T(8,128)(2,1)S(1)} %get-tuple-element.8), channel_id=1, source_target_pairs={{0,8},{8,16},{16,24},{24,0},{1,9},{9,17},{17,25},{25,1},{2,10},{10... | collective-permute-start | bytes 1572872 | tf_op jit(solution)/shard_map/ppermute | solution.py:101
  249.8 12.2 %collective-permute-start.29 = (bf16[128,2048]{1,0:T(8,128)(2,1)S(1)}, bf16[128,2048]{1,0:T(8,128)(2,1)S(1)}, u32[]{:S(2)}, u32[]{:S(2)}) collective-permute-start(bf16[128,2048]{1,0:T(8,128)(2,1)S(1)} %collective-permute-done.28), channel_id=1, source_target_pairs={{0,8},{8,16},{16,24},{24,0},{1,9},{9,17},{17,25},{25,1},{2,10},{10... | collective-permute-start | bytes 1572872 | tf_op jit(solution)/shard_map/ppermute | solution.py:101
  262.0 19.5 %collective-permute-start.30 = (bf16[128,2048]{1,0:T(8,128)(2,1)S(1)}, bf16[128,2048]{1,0:T(8,128)(2,1)S(1)}, u32[]{:S(2)}, u32[]{:S(2)}) collective-permute-start(bf16[128,2048]{1,0:T(8,128)(2,1)S(1)} %collective-permute-done.29), channel_id=1, source_target_pairs={{0,8},{8,16},{16,24},{24,0},{1,9},{9,17},{17,25},{25,1},{2,10},{10... | collective-permute-start | bytes 1572872 | tf_op jit(solution)/shard_map/ppermute | solution.py:101
  335.9 14.7 %collective-permute-start.37 = (bf16[128,1792]{1,0:T(8,128)(2,1)}, bf16[128,1792]{1,0:T(8,128)(2,1)}, u32[]{:S(2)}, u32[]{:S(2)}) collective-permute-start(bf16[128,1792]{1,0:T(8,128)(2,1)} %convolution_convert_fusion.5), channel_id=1, source_target_pairs={{0,8},{8,16},{16,24},{24,0},{1,9},{9,17},{17,25},{25,1},{2,10},{10... | collective-permute-start | bytes 1376264 | tf_op jit(solution)/shard_map/ppermute | solution.py:101
  342.4 14.1 %collective-permute-start.24 = (f32[2]{0:T(128)S(1)}, f32[2]{0:T(128)S(1)}, u32[]{:S(2)}, u32[]{:S(2)}) collective-permute-start(f32[2]{0:T(128)S(1)} %fusion.157), channel_id=1, source_target_pairs={{0,4},{1,3},{2,6},{3,1},{4,0},{5,7},{6,2},{7,5},{8,12},{9,11},{10,... | collective-permute-start | bytes 32 | tf_op jit(solution)/shard_map/ppermute | solution.py:70
  356.4 17.6 %collective-permute-start.38 = (bf16[128,1792]{1,0:T(8,128)(2,1)S(1)}, bf16[128,1792]{1,0:T(8,128)(2,1)S(1)}, u32[]{:S(2)}, u32[]{:S(2)}) collective-permute-start(bf16[128,1792]{1,0:T(8,128)(2,1)S(1)} %fusion.13), channel_id=1, source_target_pairs={{0,8},{8,16},{16,24},{24,0},{1,9},{9,17},{17,25},{25,1},{2,10},{10... | collective-permute-start | bytes 1376264 | tf_op jit(solution)/shard_map/ppermute | solution.py:101
  376.7 12.0 %collective-permute-start.39 = (bf16[128,1792]{1,0:T(8,128)(2,1)S(1)}, bf16[128,1792]{1,0:T(8,128)(2,1)S(1)}, u32[]{:S(2)}, u32[]{:S(2)}) collective-permute-start(bf16[128,1792]{1,0:T(8,128)(2,1)S(1)} %fusion.12), channel_id=1, source_target_pairs={{0,8},{8,16},{16,24},{24,0},{1,9},{9,17},{17,25},{25,1},{2,10},{10... | collective-permute-start | bytes 1376264 | tf_op jit(solution)/shard_map/ppermute | solution.py:101
  393.3 10.0 %collective-permute-start.52 = (f32[128]{0:T(128)S(1)}, f32[128]{0:T(128)S(1)}, u32[]{:S(2)}, u32[]{:S(2)}) collective-permute-start(f32[128]{0:T(128)S(1)} %broadcast_select_fusion), channel_id=1, source_target_pairs={{0,2},{1,5},{2,0},{3,7},{4,6},{5,1},{6,4},{7,3},{8,10},{9,13},{10,... | collective-permute-start | bytes 1544 | tf_op jit(solution)/shard_map/ppermute | solution.py:70
  414.5 29.1 %collective-permute-start.40 = (bf16[128,1792]{1,0:T(8,128)(2,1)}, bf16[128,1792]{1,0:T(8,128)(2,1)}, u32[]{:S(2)}, u32[]{:S(2)}) collective-permute-start(bf16[128,1792]{1,0:T(8,128)(2,1)} %get-tuple-element.14), channel_id=1, source_target_pairs={{0,8},{8,16},{16,24},{24,0},{1,9},{9,17},{17,25},{25,1},{2,10},{10... | collective-permute-start | bytes 1376264 | tf_op jit(solution)/shard_map/ppermute | solution.py:101
  414.6 11.2 %collective-permute-start.55 = (f32[4,128]{1,0:T(4,128)S(1)}, f32[4,128]{1,0:T(4,128)S(1)}, u32[]{:S(2)}, u32[]{:S(2)}) collective-permute-start(f32[4,128]{1,0:T(4,128)S(1)} %dynamic_update_slice.117), channel_id=1, source_target_pairs={{0,8},{8,0},{16,24},{24,16},{1,9},{9,1},{17,25},{25,17},{2,10},{10... | collective-permute-start | bytes 6152 | tf_op jit(solution)/shard_map/ppermute | solution.py:131
  422.5 17.0 %collective-permute-start.41 = (bf16[128,1792]{1,0:T(8,128)(2,1)}, bf16[128,1792]{1,0:T(8,128)(2,1)}, u32[]{:S(2)}, u32[]{:S(2)}) collective-permute-start(bf16[128,1792]{1,0:T(8,128)(2,1)} %get-tuple-element.12), channel_id=1, source_target_pairs={{0,8},{8,16},{16,24},{24,0},{1,9},{9,17},{17,25},{25,1},{2,10},{10... | collective-permute-start | bytes 1376264 | tf_op jit(solution)/shard_map/ppermute | solution.py:101
  425.8 11.1 %collective-permute-start.56 = (f32[4,128]{1,0:T(4,128)S(1)}, f32[4,128]{1,0:T(4,128)S(1)}, u32[]{:S(2)}, u32[]{:S(2)}) collective-permute-start(f32[4,128]{1,0:T(4,128)S(1)} %add.452), channel_id=1, source_target_pairs={{0,16},{8,24},{16,0},{24,8},{1,17},{9,25},{17,1},{25,9},{2,18},{10... | collective-permute-start | bytes 6152 | tf_op jit(solution)/shard_map/ppermute | solution.py:131
  439.5 15.4 %collective-permute-start.43 = (bf16[128,1792]{1,0:T(8,128)(2,1)}, bf16[128,1792]{1,0:T(8,128)(2,1)S(1)}, u32[]{:S(2)}, u32[]{:S(2)}) collective-permute-start(bf16[128,1792]{1,0:T(8,128)(2,1)} %collective-permute-done.41), channel_id=1, source_target_pairs={{0,8},{8,16},{16,24},{24,0},{1,9},{9,17},{17,25},{25,1},{2,10},{10... | collective-permute-start | bytes 1376264 | tf_op jit(solution)/shard_map/ppermute | solution.py:101
  443.6 21.1 %collective-permute-start.42 = (bf16[128,1792]{1,0:T(8,128)(2,1)}, bf16[128,1792]{1,0:T(8,128)(2,1)S(1)}, u32[]{:S(2)}, u32[]{:S(2)}) collective-permute-start(bf16[128,1792]{1,0:T(8,128)(2,1)} %collective-permute-done.40), channel_id=1, source_target_pairs={{0,8},{8,16},{16,24},{24,0},{1,9},{9,17},{17,25},{25,1},{2,10},{10... | collective-permute-start | bytes 1376264 | tf_op jit(solution)/shard_map/ppermute | solution.py:101
  454.9 19.7 %collective-permute-start.45 = (bf16[128,1792]{1,0:T(8,128)(2,1)S(1)}, bf16[128,1792]{1,0:T(8,128)(2,1)S(1)}, u32[]{:S(2)}, u32[]{:S(2)}) collective-permute-start(bf16[128,1792]{1,0:T(8,128)(2,1)S(1)} %collective-permute-done.43), channel_id=1, source_target_pairs={{0,8},{8,16},{16,24},{24,0},{1,9},{9,17},{17,25},{25,1},{2,10},{10... | collective-permute-start | bytes 1376264 | tf_op jit(solution)/shard_map/ppermute | solution.py:101
  464.8 18.3 %collective-permute-start.44 = (bf16[128,1792]{1,0:T(8,128)(2,1)S(1)}, bf16[128,1792]{1,0:T(8,128)(2,1)S(1)}, u32[]{:S(2)}, u32[]{:S(2)}) collective-permute-start(bf16[128,1792]{1,0:T(8,128)(2,1)S(1)} %collective-permute-done.42), channel_id=1, source_target_pairs={{0,8},{8,16},{16,24},{24,0},{1,9},{9,17},{17,25},{25,1},{2,10},{10... | collective-permute-start | bytes 1376264 | tf_op jit(solution)/shard_map/ppermute | solution.py:101
  489.2 10.7 %collective-permute-start.46 = (f32[2048]{0:T(1024)S(1)}, f32[2048]{0:T(1024)S(1)}, u32[]{:S(2)}, u32[]{:S(2)}) collective-permute-start(f32[2048]{0:T(1024)S(1)} %fusion.2), channel_id=1, source_target_pairs={{0,2},{1,5},{2,0},{3,7},{4,6},{5,1},{6,4},{7,3},{8,10},{9,13},{10,... | collective-permute-start | bytes 24584 | tf_op jit(solution)/shard_map/ppermute | solution.py:70
  491.2 12.4 %collective-permute-start.50 = (bf16[128,2048]{1,0:T(8,128)(2,1)S(1)}, bf16[128,2048]{1,0:T(8,128)(2,1)S(1)}, u32[]{:S(2)}, u32[]{:S(2)}) collective-permute-start(bf16[128,2048]{1,0:T(8,128)(2,1)S(1)} %slice.363), channel_id=1, source_target_pairs={{0,4},{1,3},{2,6},{3,1},{4,0},{5,7},{6,2},{7,5},{8,12},{9,11},{10,... | collective-permute-start | bytes 1572872 | tf_op jit(solution)/shard_map/ppermute | solution.py:64
  (76 other events, 808.3 us)
